TPU v7x, 128 devices: a whole 4x4x4 slice. The times are simulated.
128 devices in a mesh: ctx: 16 (over z, x_lo, core), fsdp: 8 (over x_hi, y).
Axes of the slice: x: 4 (x_hi: 2, x_lo: 2; x = x_hi * 2 + x_lo), y: 4, z: 4, core: 2. Of those that a mesh axis runs over, the one named last changes fastest.
Arguments:
- inputs: bfloat16 [8192, 5376], P('ctx'), may hold values from -400 to 400
- output_cotangent: bfloat16 [8192, 4096], P('ctx', 'fsdp'), may hold values from -96 to 96
- w_query: bfloat16 [5376, 4096], P('ctx', 'fsdp'), may hold values from -0.078125 to 0.078125
- key_projection: bfloat16 [5376, 2048], P('ctx', 'fsdp'), may hold values from -0.078125 to 0.078125
- value_projection: bfloat16 [5376, 2048], P('ctx', 'fsdp'), may hold values from -0.078125 to 0.078125
- norm_gain: float32 [5376], replicated, may hold values from 0.25 to 1.75
- q_gain: float32 [128], replicated, may hold values from 0.25 to 1.75
- key_norm_gain: float32 [128], replicated, may hold values from 0.25 to 1.75
- half_lengths: int32 [4], replicated, may hold values from 1 to 6144, 8192 in all
Outputs:
- grad_inputs: bfloat16 [8192, 5376], P('ctx', 'fsdp')
- grad_w_query: bfloat16 [5376, 4096], P('ctx', 'fsdp')
- grad_w_key: bfloat16 [5376, 2048], P('ctx', 'fsdp')
- grad_w_value: bfloat16 [5376, 2048], P('ctx', 'fsdp')
- grad_norm_gain: float32 [5376], P(('fsdp', 'ctx'))
- grad_q_gain: float32 [128], replicated
- grad_k_gain: float32 [128], replicated
- norm_row_dots: float32 [8192], P('ctx')
Inputs may be any that keep to these rules, and one draw needn't show every extreme that they name: `half_lengths`: the halves add up to 8192 tokens, and the longest holds exactly 6144.
All inputs are finite; a program needn't handle non-finite values.
Results may differ from a plain program's by a relative error of at most 0.035.
Values may be sent and summed in bfloat16 or wider, within the bound.
A program may use at most 128 MiB of HBM per device.

v0:
```python
import jax
import jax.numpy as jnp
from jax import lax
from jax.experimental import pallas as pl
from jax.experimental.pallas import tpu as pltpu
from jax.sharding import PartitionSpec as P

WIN = 1024
REACH = 2


epsilon = 1e-06
query_scale = 168.0 ** (-0.5)


F32, BF16 = jnp.float32, jnp.bfloat16
NT = (((1,), (1,)), ((), ()))
TN = (((0,), (0,)), ((), ()))
LOG2E = 1.4426950408889634


def attention_kernel(q_ref, kv_ref, do_ref, lo_ref, dq_ref, dkv_ref, v_one, e_all, mask, dkey, dval):
    tokens = q_ref.shape[0]
    half = tokens // 2
    span = 5 * half
    head = 128
    kvs = kv_ref.shape[1] // 2
    kv_heads = kvs // head
    group = q_ref.shape[1] // kvs
    ones = jnp.ones((kv_ref.shape[0], head), BF16)
    for g in range(kv_heads):
        v_one[g, :, :head] = kv_ref[:, kvs + g * head : kvs + (g + 1) * head]
        v_one[g, :, head:] = ones
    for t in range(2):
        col = lax.broadcasted_iota(jnp.int32, (half, span), 1) + t * half
        row = lax.broadcasted_iota(jnp.int32, (half, span), 0) + t * half
        low = lo_ref[t * half : (t + 1) * half, :]
        seen = (col >= low) & (col <= row + 2 * tokens)
        mask[t] = jnp.where(seen, 1.0, 0.0).astype(BF16)
    lane = lax.broadcasted_iota(jnp.int32, (half, head), 1)
    for g in range(kv_heads):
        dkey[...] = jnp.zeros_like(dkey)
        dval[...] = jnp.zeros_like(dval)
        for r in range(group):
            h = g * group + r
            hc = slice(h * head, (h + 1) * head)
            for t in range(2):
                qs = slice(t * half, (t + 1) * half)
                ks = slice(t * half, t * half + span)
                q = q_ref[qs, hc]
                keys = kv_ref[ks, g * head : (g + 1) * head]
                s = lax.dot_general(q, keys, NT, preferred_element_type=F32)
                e_all[...] = jnp.exp2(s).astype(BF16) * mask[t]
                out = jnp.dot(e_all[...], v_one[g, ks, :], preferred_element_type=F32)
                inv = 1.0 / out[:, head:]
                scaled = do_ref[qs, hc].astype(F32) * inv
                delta = jnp.sum(scaled * (out[:, :head] * inv), axis=1, keepdims=True)
                d_hi = delta.astype(BF16).astype(F32)
                tail = jnp.where(lane == 0, -d_hi, jnp.where(lane == 1, d_hi - delta, 0.0))
                scaled16 = scaled.astype(BF16)
                both = jnp.concatenate([scaled16, tail.astype(BF16)], axis=1)
                dp = lax.dot_general(both, v_one[g, ks, :], NT, preferred_element_type=F32)
                ds = dp.astype(BF16) * e_all[...]
                dq_ref[qs, hc] = jnp.dot(ds, keys, preferred_element_type=F32)
                dkey[ks, :] += lax.dot_general(ds, q, TN, preferred_element_type=F32)
                dval[ks, :] += lax.dot_general(e_all[...], scaled16, TN, preferred_element_type=F32)
        dkv_ref[:, g * head : (g + 1) * head] = dkey[...] * (1.0 / LOG2E)
        dkv_ref[:, kvs + g * head : kvs + (g + 1) * head] = dval[...]


def attention(q, kv, do, lo):
    tokens = q.shape[0]
    reach = kv.shape[0]
    half = tokens // 2
    vm = pl.BlockSpec(memory_space=pltpu.VMEM)
    return pl.pallas_call(
        attention_kernel,
        out_shape=(
            jax.ShapeDtypeStruct(q.shape, F32),
            jax.ShapeDtypeStruct(kv.shape, F32),
        ),
        in_specs=[vm] * 4,
        out_specs=(vm, vm),
        scratch_shapes=[
            pltpu.VMEM((kv.shape[1] // 256, reach, 256), BF16),
            pltpu.VMEM((half, 5 * half), BF16),
            pltpu.VMEM((2, half, 5 * half), BF16),
            pltpu.VMEM((reach, 128), F32),
            pltpu.VMEM((reach, 128), F32),
        ],
        compiler_params=pltpu.CompilerParams(vmem_limit_bytes=48 << 20),
        name="attention",
    )(q, kv, do, lo)


def from_behind(value, axis, steps):
    count = lax.axis_size(axis)
    initial, last = (max(0, -steps), min(count, count - steps))
    return lax.ppermute(value, axis, [(source, source + steps) for source in range(initial, last)])


def head_normalize(projected, head_count, head_dim):
    shaped = projected.reshape(projected.shape[0], head_count, head_dim)
    inverse = lax.rsqrt(jnp.mean(shaped * shaped, axis=2, keepdims=True) + epsilon)
    return (shaped * inverse, inverse)


def head_normalize_backward(upstream_grad, normal_part, inverse, gain_vector):
    upstream = upstream_grad * gain_vector
    return inverse * (
        upstream - normal_part * jnp.mean(upstream * normal_part, axis=2, keepdims=True)
    )


def on_device(
    inputs,
    output_cotangent,
    w_query,
    key_projection,
    value_projection,
    norm_gain,
    q_gain,
    key_norm_gain,
    half_lengths,
):
    tokens = inputs.shape[0]
    model_width = inputs.shape[1]
    head_dim = q_gain.shape[0]
    q_cols = w_query.shape[1]
    kv_cols = key_projection.shape[1]
    q_heads = q_cols // head_dim
    kv_heads = kv_cols // head_dim
    queries_per_group = q_heads // kv_heads
    ctx_count = lax.axis_size("ctx")
    ctx_index = lax.axis_index("ctx")
    first_row = ctx_index * tokens
    grad_scale = float(tokens * ctx_count) ** (-0.5)
    contract_cols = (((1,), (1,)), ((), ()))
    contract_rows = (((0,), (0,)), ((), ()))
    widened = inputs.astype(jnp.float32)
    inv_rms = lax.rsqrt(jnp.mean(widened * widened, axis=1, keepdims=True) + epsilon)
    x_hat = widened * inv_rms
    normed = (x_hat * norm_gain).astype(jnp.bfloat16)
    stacked = jnp.concatenate([w_query, key_projection, value_projection], axis=1)
    projected = jnp.dot(
        normed,
        lax.all_gather(stacked, "ctx", axis=0, tiled=True),
        preferred_element_type=jnp.float32,
    )
    q_raw = projected[:, :q_cols]
    key_unnormed = projected[:, q_cols : q_cols + kv_cols]
    value_rows = projected[:, q_cols + kv_cols :].astype(jnp.bfloat16)
    query_normalized, q_inverse = head_normalize(q_raw, q_heads, head_dim)
    key_normalized, key_inverse_rms = head_normalize(key_unnormed, kv_heads, head_dim)
    query_multiplier = q_gain * query_scale
    query_rows = (
        (query_normalized * (query_multiplier * LOG2E)).astype(jnp.bfloat16).reshape(tokens, q_cols)
    )
    key_rows = (key_normalized * key_norm_gain).astype(jnp.bfloat16)
    packed_kv = jnp.concatenate([key_rows.reshape(tokens, kv_cols), value_rows], axis=1)
    remote = [from_behind(packed_kv, "ctx", offset) for offset in range(REACH, 0, -1)]
    halves = half_lengths.shape[0]
    upto = lax.iota(jnp.int32, halves)[None, :] <= lax.iota(jnp.int32, halves)[:, None]
    segment_ends = jnp.sum(jnp.where(upto, half_lengths[None, :], 0), axis=1)
    positions = first_row + lax.iota(jnp.int32, tokens)
    begun = jnp.max(jnp.where(segment_ends[None, :] <= positions[:, None], segment_ends[None, :], 0), axis=1)
    lowest = jnp.maximum(positions - (WIN - 1), begun) - (first_row - REACH * tokens)
    d_query_sum, kv_grads = attention(
        query_rows, jnp.concatenate(remote + [packed_kv], axis=0), output_cotangent, lowest[:, None]
    )
    kv_grad_total = kv_grads[REACH * tokens :]
    for offset in range(1, REACH + 1):
        part = kv_grads[(REACH - offset) * tokens : (REACH - offset + 1) * tokens]
        kv_grad_total = kv_grad_total + from_behind(
            part.astype(jnp.bfloat16), "ctx", -offset
        ).astype(jnp.float32)
    d_queries = d_query_sum.reshape(tokens, q_heads, head_dim)
    key_grads = kv_grad_total[:, :kv_cols].reshape(tokens, kv_heads, head_dim)
    dq16 = (
        head_normalize_backward(d_queries, query_normalized, q_inverse, query_multiplier)
        .reshape(tokens, q_cols)
        .astype(jnp.bfloat16)
    )
    key_grads_half16 = (
        head_normalize_backward(key_grads, key_normalized, key_inverse_rms, key_norm_gain)
        .reshape(tokens, kv_cols)
        .astype(jnp.bfloat16)
    )
    value_grads_half16 = kv_grad_total[:, kv_cols:].astype(jnp.bfloat16)
    d_stacked = jnp.concatenate([dq16, key_grads_half16, value_grads_half16], axis=1)
    head_part = lax.dot_general(
        d_stacked,
        lax.all_gather(stacked, "ctx", axis=0, tiled=True),
        contract_cols,
        preferred_element_type=jnp.float32,
    )
    fsdp_index = lax.axis_index("fsdp")
    features = model_width // lax.axis_size("fsdp")
    hat_mine = lax.dynamic_slice_in_dim(x_hat, fsdp_index * features, features, 1)
    gain_mine = lax.dynamic_slice_in_dim(norm_gain, fsdp_index * features, features, 0)
    d_mine = lax.psum_scatter(
        head_part.astype(jnp.bfloat16), "fsdp", scatter_dimension=1, tiled=True
    ).astype(jnp.float32)
    upstream = d_mine * gain_mine
    row_dot = lax.psum(
        jnp.sum(d_stacked.astype(jnp.float32) * projected, axis=1, keepdims=True), "fsdp"
    )
    grad_inputs = (inv_rms * (upstream - hat_mine * row_dot / model_width)).astype(jnp.bfloat16)
    norm_row_dots = row_dot[:, 0] * float(model_width) ** (-0.5)
    gain_term = grad_scale * jnp.sum(d_mine * hat_mine, axis=0)
    weight_term = grad_scale * lax.dot_general(
        normed, d_stacked, contract_rows, preferred_element_type=jnp.float32
    )
    weight_sum, gain_sum = (
        lax.psum_scatter(
            weight_term.astype(jnp.bfloat16), "ctx", scatter_dimension=0, tiled=True
        ).astype(jnp.float32),
        lax.psum_scatter(
            gain_term.astype(jnp.bfloat16), "ctx", scatter_dimension=0, tiled=True
        ).astype(jnp.float32),
    )
    weight_sum = weight_sum.astype(jnp.bfloat16)
    q_term = grad_scale * jnp.sum(d_queries * query_normalized * query_scale, axis=(0, 1))
    k_term = grad_scale * jnp.sum(key_grads * key_normalized, axis=(0, 1))
    grad_q_gain, grad_k_gain = lax.psum((q_term, k_term), ("ctx", "fsdp"))
    return (
        grad_inputs,
        weight_sum[:, :q_cols],
        weight_sum[:, q_cols : q_cols + kv_cols],
        weight_sum[:, q_cols + kv_cols :],
        gain_sum,
        grad_q_gain,
        grad_k_gain,
        norm_row_dots,
    )


def solution(mesh):
    placed = (
        P("ctx", None),
        P("ctx", "fsdp"),
        P("ctx", "fsdp"),
        P("ctx", "fsdp"),
        P("ctx", "fsdp"),
        P(),
        P(),
        P(),
        P(),
    )
    return jax.shard_map(
        on_device,
        mesh=mesh,
        in_specs=placed,
        out_specs=(
            P("ctx", "fsdp"),
            P("ctx", "fsdp"),
            P("ctx", "fsdp"),
            P("ctx", "fsdp"),
            P(("fsdp", "ctx")),
            P(),
            P(),
            P("ctx"),
        ),
        check_vma=False,
    )
```

profile of v0, /device:TPU:1, one launch (start us, length us, event | category | flops | bytes accessed | tf_op | source)
XLA Modules:
  0.0 410.9 jit_solution(14517255345471509771)
XLA Ops:
  7.2 2.1 pad_maximum_fusion.1
  9.3 0.0 reduce-scatter.3.cloned.1.call-start
  9.4 0.8 select_reduce_fusion.1
  10.2 0.1 select_reduce_fusion
  10.3 0.1 copy.26
  10.4 8.3 %copy.24 = bf16[512,5376]{0,1:T(8,128)(2,1)} copy(bf16[512,5376]{1,0:T(8,128)(2,1)} %param.9) | data formatting | bytes 11010048 | tf_op args[0]
  18.8 3.8 fusion
  22.6 0.1 maximum_subtract_fusion.lo_ref
  22.6 55.8 %all-gather.2.cloned.1.call-done = bf16[5376,1024]{1,0:T(8,128)(2,1)} async-done(((bf16[336,1024]{1,0:T(8,128)(2,1)}), bf16[5376,1024]{1,0:T(8,128)(2,1)}) %all-gather.2.cloned.1.call-update) | async-done | bytes 11010064 | tf_op jit(solution)/shard_map/all_gather | solution.py:147
  78.4 11.7 %fusion.1 = f32[512,1024]{1,0:T(8,128)S(1)} fusion(bf16[5376,1024]{1,0:T(8,128)(2,1)} %all-gather.2.cloned.1.call-done, f32[5376]{0:T(1024)S(1)} %copy-done.18, f32[512]{0:T(512)S(1)} %add_rsqrt_fusion.2, bf16[512,5376]{0,1:T(8,128)(2,1)} %copy.24), kind=kOutput, calls=%fused_computation.9 | convolution fusion | flops 5648154624 | bytes 18635776 | tf_op jit(solution)/shard_map/dot_general | solution.py:145
  90.2 0.9 slice.49
  91.1 1.3 reshape.110
  92.4 0.6 multiply_reduce_fusion.6
  93.1 0.6 mul.258
  93.7 0.1 multiply_convert_fusion.5
  93.8 0.9 pad_maximum_fusion.2
  94.7 3.1 collective-permute-start.1
  97.9 4.1 collective-permute-start
  102.0 1.1 slice.48
  103.0 1.6 reshape.109
  104.6 0.6 multiply_reduce_fusion.3
  105.3 0.6 mul.248
  105.9 0.1 copy-done.13
  106.0 0.3 multiply_convert_fusion.4.q_ref
  106.3 0.8 collective-permute-done.1
  107.1 8.4 %collective-permute-done = bf16[512,512]{1,0:T(8,128)(2,1)} collective-permute-done((bf16[512,512]{1,0:T(8,128)(2,1)}, bf16[512,512]{1,0:T(8,128)(2,1)}, u32[]{:S(2)}, u32[]{:S(2)}) %collective-permute-start) | collective-permute-done | bytes 524320 | tf_op jit(solution)/shard_map/ppermute | solution.py:99
  115.5 1.3 maximum_maximum_fusion.kv_ref
  116.9 13.7 %attention.1 = (f32[512,512]{1,0:T(8,128)S(1)}, f32[1536,512]{1,0:T(8,128)}) custom-call(bf16[512,512]{1,0:T(8,128)(2,1)S(1)} %multiply_convert_fusion.4.q_ref, bf16[1536,512]{1,0:T(8,128)(2,1)S(1)} %maximum_maximum_fusion.kv_ref, bf16[512,512]{1,0:T(8,128)(2,1)S(1)} %copy-done, s32[512,1]{1,0:T(8,128)S(1)} %maximum_subtract_fusion.lo_ref), custom_call_target="tpu_custom_call" | custom-call | tf_op jit(solution)/shard_map/attention/pallas_call | solution.py:76
  130.6 1.3 reshape.111
  131.9 2.8 multiply_reduce_fusion.2
  134.7 2.1 convert.11
  136.8 0.1 fusion.12
  136.9 2.1 collective-permute-start.2
  139.0 1.3 collective-permute-start.3
  140.3 0.6 mul.276
  140.9 1.3 multiply_reduce_fusion.1
  142.3 9.0 %collective-permute-done.2 = bf16[512,512]{1,0:T(8,128)(2,1)S(1)} collective-permute-done((bf16[512,512]{1,0:T(8,128)(2,1)S(1)}, bf16[512,512]{1,0:T(8,128)(2,1)S(1)}, u32[]{:S(2)}, u32[]{:S(2)}) %collective-permute-start.2) | collective-permute-done | bytes 524320 | tf_op jit(solution)/shard_map/ppermute | solution.py:99
  151.3 4.0 collective-permute-done.3
  155.3 1.4 convert_add_fusion
  156.8 0.7 slice.69
  157.5 0.8 slice.53
  158.3 2.1 reshape.112
  160.5 2.7 multiply_reduce_fusion.5
  163.2 0.6 mul.285
  163.8 0.2 multiply_reduce_fusion.4
  164.1 11.9 %convolution_convert_fusion = bf16[512,5376]{0,1:T(8,128)(2,1)} fusion(bf16[5376,1024]{1,0:T(8,128)(2,1)} %all-gather.2.cloned.1.call-done, bf16[512,256]{1,0:T(8,128)(2,1)S(1)} %copy-done.16, bf16[512,256]{1,0:T(8,128)(2,1)S(1)} %get-tuple-element.19, bf16[512,512]{1,0:T(8,128)(2,1)S(1)} %copy-done.14), kind=kOutput, calls=%fused_computation.5 | convolution fusion | flops 5643042816 | bytes 17563648 | tf_op jit(solution)/shard_map/dot_general | solution.py:191
  176.0 0.3 reduce-scatter.5.cloned.1.call-start
  176.3 0.7 copy-done.15
  177.0 0.1 copy-done.17
  177.0 11.1 %multiply_convert_fusion = bf16[5376,1024]{1,0:T(8,128)(2,1)} fusion(f32[5376]{0:T(1024)S(1)} %copy-done.18, f32[512]{0:T(512)S(1)} %add_rsqrt_fusion.2, bf16[512,5376]{0,1:T(8,128)(2,1)} %copy.24, bf16[512,256]{1,0:T(8,128)(2,1)S(1)} %copy-done.17, bf16[512,256]{1,0:T(8,128)(2,1)S(1)} %get-tuple-element.19, bf16[512,512]{1,0:T(8,128)(2,1)S(1)} %copy-done.15), kind=kOutput, calls=%fused_computation | convolution fusion | flops 5662310400 | bytes 17587200 | tf_op jit(solution)/shard_map/dot_general | solution.py:211
  188.2 0.1 dynamic_slice.6
  188.3 0.5 copy-done.21
  188.8 0.6 dynamic-slice
  190.1 8.7 %convert_multiply_fusion = f32[512,5376]{0,1:T(8,128)} fusion(bf16[512,5376]{0,1:T(8,128)(2,1)} %copy.24, f32[512]{0:T(512)S(1)} %add_rsqrt_fusion.2), kind=kLoop, calls=%fused_computation.1 | loop fusion | flops 5505024 | bytes 16517120 | tf_op jit(solution)/shard_map/mul | solution.py:142
  198.8 77.4 %all-reduce.1 = (f32[128]{0:T(128)}, f32[128]{0:T(128)}) all-reduce(f32[128]{0:T(128)S(1)} %get-tuple-element.27, f32[128]{0:T(128)S(1)} %get-tuple-element.26), channel_id=1, replica_groups=mesh['ctx'=16,'fsdp'=8] {'ctx','fsdp'}, use_global_device_ids=true, to_apply=%region_15.16 | all-reduce | flops 256 | bytes 2048 | tf_op jit(solution)/shard_map/psum | solution.py:225
  276.2 0.3 multiply_reduce_fusion
  276.4 17.6 %psum.21 = f32[512]{0:T(512)S(1)} all-reduce(f32[512]{0:T(512)S(1)} %multiply_reduce_fusion), channel_id=1, replica_groups=mesh['ctx'=16,'fsdp'=8] {'fsdp'}, use_global_device_ids=true, to_apply=%region_9.10 | all-reduce | flops 512 | bytes 4096 | tf_op jit(solution)/shard_map/psum | solution.py:205
  294.1 0.6 broadcast_multiply_fusion.2
  294.7 3.0 fusion.5
  297.6 32.1 %all-reduce = bf16[672]{0:T(1024)(128)(2,1)S(1)} all-reduce(bf16[672]{0:T(1024)(128)(2,1)S(1)} %multiply_convert_fusion.6), channel_id=4, replica_groups=mesh['ctx'=16,'fsdp'=8] {'ctx'}, use_global_device_ids=true, to_apply=%region_12.13.clone | all-reduce | flops 672 | bytes 2688
  329.8 0.6 dynamic-slice_convert_fusion
  330.4 70.5 %reduce-scatter.5.cloned.1.call-done = bf16[336,1024]{1,0:T(8,128)(2,1)} async-done(((bf16[5376,1024]{1,0:T(8,128)(2,1)}), bf16[336,1024]{1,0:T(8,128)(2,1)}) %reduce-scatter.5.cloned.1.call-update) | async-done | bytes 688144 | tf_op jit(solution)/shard_map/reduce_scatter | solution.py:215
  400.9 1.7 slice.55
  402.6 1.8 fusion.13
  (60 shorter events, 0.4 us)
Async XLA Ops:
  7.2 71.3 %all-gather.2.cloned.1.call-start = ((), (), s32[]{:S(2)}) async-start(), calls=%async_computation.2 | async-start | bytes 11698176 | tf_op jit(solution)/shard_map/all_gather | solution.py:147
  9.3 285.3 %reduce-scatter.3.cloned.1.call-start = ((), (), s32[]{:S(2)}) async-start(), calls=%async_computation.3 | async-start | bytes 6193152 | tf_op jit(solution)/shard_map/reduce_scatter | solution.py:201
  10.4 8.3 %copy-start.19 = (f32[128]{0:T(128)S(1)}, f32[128]{0:T(128)}, u32[]{:S(2)}) copy-start(f32[128]{0:T(128)} %param.16) | copy-start | bytes 1540
  10.4 8.3 %copy-start.20 = (f32[128]{0:T(128)S(1)}, f32[128]{0:T(128)}, u32[]{:S(2)}) copy-start(f32[128]{0:T(128)} %param.15) | copy-start | bytes 1540
  18.8 59.7 %copy-start.18 = (f32[5376]{0:T(1024)S(1)}, f32[5376]{0:T(1024)}, u32[]{:S(2)}) copy-start(f32[5376]{0:T(1024)} %param.14) | copy-start | bytes 64516
  90.2 4.5 %copy-start.9 = (bf16[512,256]{1,0:T(8,128)(2,1)}, bf16[512,256]{1,0:T(8,128)(2,1)S(1)}, u32[]{:S(2)}) copy-start(bf16[512,256]{1,0:T(8,128)(2,1)S(1)} %slice.70) | copy-start | bytes 786436
  92.4 9.6 %copy-start.4 = (f32[512,2,128]{2,1,0:T(2,128)}, f32[512,2,128]{2,1,0:T(2,128)S(1)}, u32[]{:S(2)}) copy-start(f32[512,2,128]{2,1,0:T(2,128)S(1)} %reshape.110) | copy-start | bytes 1572868
  93.1 8.9 %copy-start.7 = (f32[512,2]{1,0:T(8,128)}, f32[512,2]{1,0:T(8,128)S(1)}, u32[]{:S(2)}) copy-start(f32[512,2]{1,0:T(8,128)S(1)} %add_rsqrt_fusion) | copy-start | bytes 12292
  93.7 8.3 %copy-start.5 = (f32[512,2,128]{2,1,0:T(2,128)}, f32[512,2,128]{2,1,0:T(2,128)S(1)}, u32[]{:S(2)}) copy-start(f32[512,2,128]{2,1,0:T(2,128)S(1)} %mul.258) | copy-start | bytes 1572868
  93.8 8.2 %copy-start.11 = (bf16[512,256]{1,0:T(8,128)(2,1)}, bf16[512,256]{1,0:T(8,128)(2,1)S(1)}, u32[]{:S(2)}) copy-start(bf16[512,256]{1,0:T(8,128)(2,1)S(1)} %multiply_convert_fusion.5) | copy-start | bytes 786436
  94.7 12.4 %collective-permute-start.1 = (bf16[512,512]{1,0:T(8,128)(2,1)}, bf16[512,512]{1,0:T(8,128)(2,1)}, u32[]{:S(2)}, u32[]{:S(2)}) collective-permute-start(bf16[512,512]{1,0:T(8,128)(2,1)} %pad_maximum_fusion.2), channel_id=1, source_target_pairs={{0,8},{8,16},{16,24},{24,32},{32,40},{40,48},{48,56},{56,64},{64,7... | collective-permute-start | bytes 1572872 | tf_op jit(solution)/shard_map/ppermute | solution.py:99
  97.9 17.7 %collective-permute-start = (bf16[512,512]{1,0:T(8,128)(2,1)}, bf16[512,512]{1,0:T(8,128)(2,1)}, u32[]{:S(2)}, u32[]{:S(2)}) collective-permute-start(bf16[512,512]{1,0:T(8,128)(2,1)} %pad_maximum_fusion.2), channel_id=1, source_target_pairs={{0,16},{8,24},{16,32},{24,40},{32,48},{40,56},{48,64},{56,72},{64,... | collective-permute-start | bytes 1572872 | tf_op jit(solution)/shard_map/ppermute | solution.py:99
  104.6 10.9 %copy-start.1 = (f32[512,4,128]{2,1,0:T(4,128)}, f32[512,4,128]{2,1,0:T(4,128)S(1)}, u32[]{:S(2)}) copy-start(f32[512,4,128]{2,1,0:T(4,128)S(1)} %reshape.109) | copy-start | bytes 3145732
  104.6 10.9 %copy-start.10 = (bf16[512,256]{1,0:T(8,128)(2,1)S(1)}, bf16[512,256]{1,0:T(8,128)(2,1)}, u32[]{:S(2)}) copy-start(bf16[512,256]{1,0:T(8,128)(2,1)} %copy-done.9) | copy-start | bytes 786436
  104.6 10.9 %copy-start.12 = (bf16[512,256]{1,0:T(8,128)(2,1)S(1)}, bf16[512,256]{1,0:T(8,128)(2,1)}, u32[]{:S(2)}) copy-start(bf16[512,256]{1,0:T(8,128)(2,1)} %copy-done.11) | copy-start | bytes 786436
  105.3 0.7 copy-start.13
  106.0 1.1 copy-start.2
  106.0 10.8 %copy-start = (bf16[512,512]{1,0:T(8,128)(2,1)S(1)}, bf16[512,512]{1,0:T(8,128)(2,1)}, u32[]{:S(2)}) copy-start(bf16[512,512]{1,0:T(8,128)(2,1)} %do_ref.1) | copy-start | bytes 1572868
  136.8 4.1 copy-start.3
  136.9 14.4 %collective-permute-start.2 = (bf16[512,512]{1,0:T(8,128)(2,1)S(1)}, bf16[512,512]{1,0:T(8,128)(2,1)S(1)}, u32[]{:S(2)}, u32[]{:S(2)}) collective-permute-start(bf16[512,512]{1,0:T(8,128)(2,1)S(1)} %get-tuple-element.20), channel_id=1, source_target_pairs={{8,0},{16,8},{24,16},{32,24},{40,32},{48,40},{56,48},{64,56},{72,6... | collective-permute-start | bytes 1572872 | tf_op jit(solution)/shard_map/ppermute | solution.py:99
  139.0 16.4 %collective-permute-start.3 = (bf16[512,512]{1,0:T(8,128)(2,1)S(1)}, bf16[512,512]{1,0:T(8,128)(2,1)S(1)}, u32[]{:S(2)}, u32[]{:S(2)}) collective-permute-start(bf16[512,512]{1,0:T(8,128)(2,1)S(1)} %get-tuple-element.21), channel_id=1, source_target_pairs={{16,0},{24,8},{32,16},{40,24},{48,32},{56,40},{64,48},{72,56},{80,... | collective-permute-start | bytes 1572872 | tf_op jit(solution)/shard_map/ppermute | solution.py:99
  142.3 18.2 %copy-start.8 = (f32[512,2]{1,0:T(8,128)S(1)}, f32[512,2]{1,0:T(8,128)}, u32[]{:S(2)}) copy-start(f32[512,2]{1,0:T(8,128)} %copy-done.7) | copy-start | bytes 12292
  160.5 3.4 copy-start.6
  160.5 3.6 copy-start.14
  160.5 3.6 copy-start.16
  175.9 1.0 copy-start.15
  175.9 1.1 copy-start.17
  176.0 224.9 %reduce-scatter.5.cloned.1.call-start = ((), (), s32[]{:S(2)}) async-start(), calls=%async_computation.4 | async-start | bytes 11698176 | tf_op jit(solution)/shard_map/reduce_scatter | solution.py:215
  188.2 0.7 copy-start.21
Sparse Core Ops, SparseCore 0:
  10.3 68.1 all-gather.1
  176.1 99.4 reduce-scatter.2
  278.2 122.6 reduce-scatter.4
where the time goes:
time: 413 us; the launch traced here: 411 us
  waiting for transfers between devices  149 us (36%)
  blocking collectives  127 us (31%)
  matrix products  34.7 us (8%)
  other arithmetic  34.4 us (8%)
  local copies, waits for them, and re-layouts  26.4 us (6%)
  between operations  14.8 us (4%)
  Pallas kernels  13.7 us (3%)
  starting transfers between devices  10.9 us (3%)
    psum x1, blocking collectives, on_device(): grad_q_gain, grad_k_gain = lax.psum((q_term, k_term), ('ctx', 'fsdp'))  77.4 us
    reduce_scatter x1, waiting for transfers between devices, on_device(): lax.psum_scatter(weight_term.astype(jnp.bfloat16), 'ctx', scatter_dimensi...  70.5 us
    all_gather x1, waiting for transfers between devices, on_device(): lax.all_gather(stacked, 'ctx', axis=0, tiled=True)  55.8 us
    unnamed x1, blocking collectives  32.1 us
    ppermute x4, waiting for transfers between devices, from_behind(): lax.ppermute(value, axis, [(source, source + steps) for source in range(i...  22.3 us
    psum x1, blocking collectives, on_device(): lax.psum(jnp.sum(d_stacked.astype(jnp.float32) * projected, axis=1, keepd...  17.6 us
    pallas_call x1, Pallas kernels, attention(): pl.pallas_call(attention_kernel, out_shape=(jax.ShapeDtypeStruct(q.shape,...  13.7 us
    dot_general x1, matrix products, on_device(): lax.dot_general(d_stacked, lax.all_gather(stacked, 'ctx', axis=0, tiled=T...  11.9 us
  transfers between devices with their start and end apart: 7, of which 6 were waited for; matrix products, arithmetic and copies ran while one was open for 11% of the time, Pallas kernels for 0%

commit v1 on v0

--- a/solution.py
+++ b/solution.py
@@ -16,6 +16,7 @@
 F32, BF16 = jnp.float32, jnp.bfloat16
 NT = (((1,), (1,)), ((), ()))
 TN = (((0,), (0,)), ((), ()))
+MESH = pl.DeviceIdType.MESH
 LOG2E = 1.4426950408889634
 
 
@@ -92,6 +93,155 @@
         name="attention",
     )(q, kv, do, lo)
 
+def both_reductions(w_ref, nt_ref, d_ref, scale):
+    blocks, wide, cols = w_ref.shape
+    tokens = d_ref.shape[0]
+    part = wide // 2
+    wing = cols // 2
+
+    def kernel(w, nt, d, dn_out, wg_out, nt_far, d_far, far, near, half_in, near_in, cross, cross_in,
+               swap_s, swap_r, half_s, half_r, near_s, near_r, cross_s, cross_r):
+        c, f = lax.axis_index("ctx"), lax.axis_index("fsdp")
+        z, x, core = c // 4, lax.rem(c // 2, 2), lax.rem(c, 2)
+        xh, y = f // 4, lax.rem(f, 4)
+        ring = (
+            lambda k: (c, xh * 4 + lax.rem(y + k, 4)),
+            lambda k: (lax.rem(z + k, 4) * 4 + x * 2 + core, f),
+        )
+        across = ((c, (1 - xh) * 4 + y), (z * 4 + (1 - x) * 2 + core, f))
+        twin = (z * 4 + x * 2 + 1 - core, f)
+
+        barrier = pltpu.get_barrier_semaphore()
+        partners = [twin, *across] + [ring[m](k) for m in range(2) for k in (1, 3)]
+        for partner in partners:
+            pl.semaphore_signal(barrier, inc=1, device_id=partner, device_id_type=MESH)
+        pl.semaphore_wait(barrier, len(partners))
+
+        def copy(src, dst, ss, rs, to):
+            return pltpu.make_async_remote_copy(
+                src_ref=src, dst_ref=dst, send_sem=ss, recv_sem=rs, device_id=to, device_id_type=MESH
+            )
+
+        swaps = [
+            copy(d, d_far, swap_s.at[0], swap_r.at[0], twin),
+            copy(nt.at[:, 1 - core], nt_far, swap_s.at[1], swap_r.at[1], twin),
+        ]
+        for swap in swaps:
+            swap.start()
+
+        def term(m, s, k, h):
+            if m == 0:
+                block = (xh if s else 1 - xh) * 4 + lax.rem(y + k, 4)
+                rows = w[block, h * part : (h + 1) * part, :]
+                return lax.dot_general(rows, d[...], NT, preferred_element_type=F32)
+            block = lax.rem(z + k, 4) * 2 + (x if s else 1 - x)
+            hs = slice(h * wing, (h + 1) * wing)
+            total = jnp.dot(nt[block, core], d[:, hs], preferred_element_type=F32)
+            total += jnp.dot(nt_far[block], d_far[:, hs], preferred_element_type=F32)
+            return total * scale
+
+        sent = []
+
+        def send_far(m, s):
+            for h in range(2):
+                far[m, s, h] = term(m, s, 2, h).astype(BF16)
+                cp = copy(far.at[m, s, h], half_in.at[m, s, h], half_s.at[m, s, h], half_r.at[m, s, h],
+                          ring[m](1 if h == 0 else 3))
+                cp.start()
+                sent.append(cp)
+                halves[m, s, h] = cp
+
+        def make_near(m, s):
+            for n, k in enumerate((1, 3)):
+                for h in range(2):
+                    near[m, s, n, h] = term(m, s, k, h).astype(BF16)
+
+        def send_near(m, s):
+            for n, k in enumerate((1, 3)):
+                halves[m, s, n].wait_recv()
+                near[m, s, n, n] = (near[m, s, n, n].astype(F32) + half_in[m, s, n].astype(F32)).astype(BF16)
+                cp = copy(near.at[m, s, n], near_in.at[m, s, n], near_s.at[m, s, n], near_r.at[m, s, n], ring[m](k))
+                cp.start()
+                sent.append(cp)
+                nears[m, s, n] = cp
+
+        def arrived(m, s, h):
+            return near_in[m, s, 0, h].astype(F32) + near_in[m, s, 1, h].astype(F32)
+
+        halves, nears, crossed = {}, {}, {}
+        send_far(0, 0)
+        make_near(0, 0)
+        for swap in swaps:
+            swap.wait_recv()
+        send_far(1, 0)
+        send_near(0, 0)
+        make_near(1, 0)
+        send_far(0, 1)
+        send_near(1, 0)
+        send_far(1, 1)
+        make_near(0, 1)
+        send_near(0, 1)
+        make_near(1, 1)
+        send_near(1, 1)
+        for m in range(2):
+            for h in range(2):
+                if h == 0:
+                    mine = [term(m, 0, 0, 0), term(m, 0, 0, 1)]
+                    for n in range(2):
+                        nears[m, 0, n].wait_recv()
+                cross[m, h] = (mine[h] + arrived(m, 0, h)).astype(BF16)
+            cp = copy(cross.at[m], cross_in.at[m], cross_s.at[m], cross_r.at[m], across[m])
+            cp.start()
+            sent.append(cp)
+            crossed[m] = cp
+        for h in range(2):
+            dn_out[h] = term(0, 1, 0, h)
+        weights = [term(1, 1, 0, h) for h in range(2)]
+        for n in range(2):
+            nears[0, 1, n].wait_recv()
+        crossed[0].wait_recv()
+        for h in range(2):
+            dn_out[h] = dn_out[h] + arrived(0, 1, h) + cross_in[0, h].astype(F32)
+        for n in range(2):
+            nears[1, 1, n].wait_recv()
+        crossed[1].wait_recv()
+        for h in range(2):
+            total = weights[h] + arrived(1, 1, h) + cross_in[1, h].astype(F32)
+            wg_out[:, h * wing : (h + 1) * wing] = total.astype(BF16)
+        for cp in swaps + sent:
+            cp.wait_send()
+
+    vm = pl.BlockSpec(memory_space=pltpu.VMEM)
+    dma = pltpu.SemaphoreType.DMA
+    block = (2, part, tokens)
+    return pl.pallas_call(
+        kernel,
+        out_shape=(
+            jax.ShapeDtypeStruct(block, F32),
+            jax.ShapeDtypeStruct((part, cols), BF16),
+        ),
+        in_specs=[vm] * 3,
+        out_specs=(vm, vm),
+        scratch_shapes=[
+            pltpu.VMEM((blocks, part, tokens), BF16),
+            pltpu.VMEM((tokens, cols), BF16),
+            pltpu.VMEM((2, 2) + block, BF16),
+            pltpu.VMEM((2, 2, 2) + block, BF16),
+            pltpu.VMEM((2, 2) + block, BF16),
+            pltpu.VMEM((2, 2, 2) + block, BF16),
+            pltpu.VMEM((2,) + block, BF16),
+            pltpu.VMEM((2,) + block, BF16),
+            dma((2,)), dma((2,)),
+            dma((2, 2, 2)), dma((2, 2, 2)),
+            dma((2, 2, 2)), dma((2, 2, 2)),
+            dma((2,)), dma((2,)),
+        ],
+        compiler_params=pltpu.CompilerParams(
+            collective_id=1, has_side_effects=True, vmem_limit_bytes=60 << 20
+        ),
+        name="both_reductions",
+    )(w_ref, nt_ref, d_ref)
+
 
 def from_behind(value, axis, steps):
     count = lax.axis_size(axis)
@@ -135,16 +285,15 @@
     ctx_index = lax.axis_index("ctx")
     first_row = ctx_index * tokens
     grad_scale = float(tokens * ctx_count) ** (-0.5)
-    contract_cols = (((1,), (1,)), ((), ()))
-    contract_rows = (((0,), (0,)), ((), ()))
     widened = inputs.astype(jnp.float32)
     inv_rms = lax.rsqrt(jnp.mean(widened * widened, axis=1, keepdims=True) + epsilon)
     x_hat = widened * inv_rms
     normed = (x_hat * norm_gain).astype(jnp.bfloat16)
     stacked = jnp.concatenate([w_query, key_projection, value_projection], axis=1)
+    gathered = lax.all_gather(stacked, "ctx", axis=0, tiled=True)
     projected = jnp.dot(
         normed,
-        lax.all_gather(stacked, "ctx", axis=0, tiled=True),
+        gathered,
         preferred_element_type=jnp.float32,
     )
     q_raw = projected[:, :q_cols]
@@ -188,38 +337,31 @@
     )
     value_grads_half16 = kv_grad_total[:, kv_cols:].astype(jnp.bfloat16)
     d_stacked = jnp.concatenate([dq16, key_grads_half16, value_grads_half16], axis=1)
-    head_part = lax.dot_general(
+    fsdp_index = lax.axis_index("fsdp")
+    fsdp_count = lax.axis_size("fsdp")
+    features = model_width // fsdp_count
+    inputs_t = inputs.T
+    inv_row = inv_rms.reshape(1, tokens)
+    normed_t = (inputs_t.astype(jnp.float32) * inv_row * norm_gain[:, None]).astype(jnp.bfloat16)
+    hat_mine = (
+        lax.dynamic_slice_in_dim(inputs_t, fsdp_index * features, features, 0).astype(jnp.float32) * inv_row
+    )
+    gain_mine = lax.dynamic_slice_in_dim(norm_gain, fsdp_index * features, features, 0)
+    d_mine, weight_sum = both_reductions(
+        gathered.reshape(fsdp_count, features, -1),
+        normed_t.reshape(ctx_count // 2, 2, model_width // ctx_count, tokens),
         d_stacked,
-        lax.all_gather(stacked, "ctx", axis=0, tiled=True),
-        contract_cols,
-        preferred_element_type=jnp.float32,
-    )
-    fsdp_index = lax.axis_index("fsdp")
-    features = model_width // lax.axis_size("fsdp")
-    hat_mine = lax.dynamic_slice_in_dim(x_hat, fsdp_index * features, features, 1)
-    gain_mine = lax.dynamic_slice_in_dim(norm_gain, fsdp_index * features, features, 0)
-    d_mine = lax.psum_scatter(
-        head_part.astype(jnp.bfloat16), "fsdp", scatter_dimension=1, tiled=True
+        grad_scale,
+    )
+    d_mine = d_mine.reshape(features, tokens)
+    row_dot = lax.psum(jnp.sum(d_stacked.astype(jnp.float32) * projected, axis=1), "fsdp")
+    upstream = d_mine * gain_mine[:, None]
+    grad_inputs = (inv_row * (upstream - hat_mine * (row_dot[None, :] / model_width))).astype(jnp.bfloat16).T
+    norm_row_dots = row_dot * float(model_width) ** (-0.5)
+    gain_term = grad_scale * jnp.sum(d_mine * hat_mine, axis=1)
+    gain_sum = lax.psum_scatter(
+        gain_term.astype(jnp.bfloat16), "ctx", scatter_dimension=0, tiled=True
     ).astype(jnp.float32)
-    upstream = d_mine * gain_mine
-    row_dot = lax.psum(
-        jnp.sum(d_stacked.astype(jnp.float32) * projected, axis=1, keepdims=True), "fsdp"
-    )
-    grad_inputs = (inv_rms * (upstream - hat_mine * row_dot / model_width)).astype(jnp.bfloat16)
-    norm_row_dots = row_dot[:, 0] * float(model_width) ** (-0.5)
-    gain_term = grad_scale * jnp.sum(d_mine * hat_mine, axis=0)
-    weight_term = grad_scale * lax.dot_general(
-        normed, d_stacked, contract_rows, preferred_element_type=jnp.float32
-    )
-    weight_sum, gain_sum = (
-        lax.psum_scatter(
-            weight_term.astype(jnp.bfloat16), "ctx", scatter_dimension=0, tiled=True
-        ).astype(jnp.float32),
-        lax.psum_scatter(
-            gain_term.astype(jnp.bfloat16), "ctx", scatter_dimension=0, tiled=True
-        ).astype(jnp.float32),
-    )
-    weight_sum = weight_sum.astype(jnp.bfloat16)
     q_term = grad_scale * jnp.sum(d_queries * query_normalized * query_scale, axis=(0, 1))
     k_term = grad_scale * jnp.sum(key_grads * key_normalized, axis=(0, 1))
     grad_q_gain, grad_k_gain = lax.psum((q_term, k_term), ("ctx", "fsdp"))

time: 413 us -> 387 us (0.937); the launches traced: 411 us -> 379 us
  Pallas kernels: 13.7 us -> 99.4 us
  waiting for transfers between devices: 149 us -> 69.3 us
  matrix products: 34.7 us -> 10.4 us
  blocking collectives: 127 us -> 115 us
  other arithmetic: 34.4 us -> 29.6 us
    pallas_call x0 -> x1, Pallas kernels: none -> 85.8 us  [both_reductions(): pl.pallas_call(kernel, out_shape=(jax.ShapeDtypeStruct(block, F32), jax.S...]
    reduce_scatter x2 -> x0, waiting for transfers between devices: 70.5 us -> none  [the longest x1 70.5 us: on_device(): lax.psum_scatter(weight_term.astype(jnp.bfloat16), 'ctx', scatter_dimensi...]
    dot_general x3 -> x1, matrix products: 34.7 us -> 10.4 us  [on_device(): projected = jnp.dot(normed, gathered, preferred_element_type=jnp.float32)]
    psum x1, blocking collectives: 77.4 us -> 62 us  [on_device(): grad_q_gain, grad_k_gain = lax.psum((q_term, k_term), ('ctx', 'fsdp'))]
    all_gather x1, waiting for transfers between devices: 55.8 us -> 47 us  [on_device(): gathered = lax.all_gather(stacked, 'ctx', axis=0, tiled=True)]
    mul x2 -> x1, other arithmetic: 9.23 us -> 0.58 us  [on_device(): norm_row_dots = row_dot * float(model_width) ** (-0.5)]
    convert_element_type x0 -> x1, local copies, waits for them, and re-layouts: none -> 8.37 us  [on_device(): (inputs_t.astype(jnp.float32) * inv_row * norm_gain[:, None]).astype(jnp....]
    unnamed x46 -> x50, local copies, waits for them, and re-layouts: 10.4 us -> 3.29 us
  transfers between devices with their start and end apart: 7 -> 5, of which waited for: 6 -> 5; matrix products, arithmetic and copies ran while one was open for 11% -> 7% of each run, Pallas kernels for 0% -> 0%
where the time goes in v1:
time: 387 us; the launch traced here: 379 us
  blocking collectives  115 us (30%)
  Pallas kernels  99.4 us (26%)
  waiting for transfers between devices  69.3 us (18%)
  other arithmetic  29.6 us (8%)
  local copies, waits for them, and re-layouts  29.5 us (8%)
  between operations  15.6 us (4%)
  matrix products  10.4 us (3%)
  starting transfers between devices  10.3 us (3%)
    pallas_call x1, Pallas kernels, both_reductions(): pl.pallas_call(kernel, out_shape=(jax.ShapeDtypeStruct(block, F32), jax.S...  85.8 us
    psum x1, blocking collectives, on_device(): grad_q_gain, grad_k_gain = lax.psum((q_term, k_term), ('ctx', 'fsdp'))  62 us
    all_gather x1, waiting for transfers between devices, on_device(): gathered = lax.all_gather(stacked, 'ctx', axis=0, tiled=True)  47 us
    unnamed x1, blocking collectives  31 us
    psum x1, blocking collectives, on_device(): lax.psum(jnp.sum(d_stacked.astype(jnp.float32) * projected, axis=1), 'fsdp')  22.4 us
    ppermute x4, waiting for transfers between devices, from_behind(): lax.ppermute(value, axis, [(source, source + steps) for source in range(i...  22.2 us
    pallas_call x1, Pallas kernels, attention(): pl.pallas_call(attention_kernel, out_shape=(jax.ShapeDtypeStruct(q.shape,...  13.6 us
    dot_general x1, matrix products, on_device(): projected = jnp.dot(normed, gathered, preferred_element_type=jnp.float32)  10.4 us
  transfers between devices with their start and end apart: 5, of which 5 were waited for; matrix products, arithmetic and copies ran while one was open for 7% of the time, Pallas kernels for 0%

profile of v1, /device:TPU:1, one launch (start us, length us, event | category | flops | bytes accessed | tf_op | source)
XLA Modules:
  0.0 379.4 jit_solution(4357333963908371045)
XLA Ops:
  7.2 0.0 all-gather.2.cloned.1.call-start
  7.2 2.1 pad_maximum_fusion.1
  9.4 0.8 select_reduce_fusion.1
  10.1 0.1 select_reduce_fusion
  10.2 0.1 copy.30
  10.4 3.9 %fusion = f32[512]{0:T(512)S(1)} fusion(bf16[512,5376]{1,0:T(8,128)(2,1)} %param.9), kind=kLoop, calls=%fused_computation.2 | loop fusion | flops 8257024 | bytes 5507072 | tf_op jit(solution)/shard_map/reduce_sum | solution.py:289
  14.3 0.3 copy-done.1
  14.6 4.3 %fusion.5 = bf16[5376,512]{0,1:T(8,128)(2,1)} fusion(f32[5376]{0:T(1024)S(1)} %copy-done.20, f32[512]{0:T(512)S(1)} %add_rsqrt_fusion.2, bf16[512,5376]{1,0:T(8,128)(2,1)S(1)} %copy-done.1), kind=kLoop, calls=%fused_computation.7 | loop fusion | flops 11010048 | bytes 11033600 | tf_op jit(solution)/shard_map/convert_element_type | solution.py:345
  18.8 8.4 %copy.28 = bf16[5376,512]{1,0:T(8,128)(2,1)} copy(bf16[5376,512]{0,1:T(8,128)(2,1)} %fusion.5) | data formatting | bytes 11010048 | tf_op jit(solution)/shard_map/convert_element_type | solution.py:345
  27.2 0.1 dynamic_slice.6
  27.3 1.6 constant_dynamic-slice_fusion
  28.9 1.1 copy.32
  30.1 0.6 dynamic-slice.1
  31.4 0.1 maximum_subtract_fusion.lo_ref
  31.4 47.0 %all-gather.2.cloned.1.call-done = bf16[5376,1024]{1,0:T(8,128)(2,1)} async-done(((bf16[336,1024]{1,0:T(8,128)(2,1)}), bf16[5376,1024]{1,0:T(8,128)(2,1)}) %all-gather.2.cloned.1.call-update) | async-done | bytes 11010064 | tf_op jit(solution)/shard_map/all_gather | solution.py:293
  78.4 10.4 %fusion.3 = f32[512,1024]{1,0:T(8,128)S(1)} fusion(bf16[5376,1024]{1,0:T(8,128)(2,1)} %all-gather.2.cloned.1.call-done, bf16[512,5376]{1,0:T(8,128)(2,1)} %param.9, f32[5376]{0:T(1024)S(1)} %copy-done.20, f32[512]{0:T(512)S(1)} %add_rsqrt_fusion.2), kind=kOutput, calls=%fused_computation.6 | convolution fusion | flops 5648154624 | bytes 18635776 | tf_op jit(solution)/shard_map/dot_general | solution.py:294
  88.8 0.8 slice.49
  89.7 1.4 reshape.130
  91.1 0.6 multiply_reduce_fusion.6
  91.8 0.6 mul.271
  92.4 0.1 multiply_convert_fusion.1
  92.5 0.9 pad_maximum_fusion.2
  93.5 3.8 %collective-permute-start = (bf16[512,512]{1,0:T(8,128)(2,1)}, bf16[512,512]{1,0:T(8,128)(2,1)}, u32[]{:S(2)}, u32[]{:S(2)}) collective-permute-start(bf16[512,512]{1,0:T(8,128)(2,1)} %pad_maximum_fusion.2), channel_id=1, source_target_pairs={{0,16},{8,24},{16,32},{24,40},{32,48},{40,56},{48,64},{56,72},{64,... | collective-permute-start | bytes 1572872 | tf_op jit(solution)/shard_map/ppermute | solution.py:249
  97.3 3.1 collective-permute-start.1
  100.4 1.1 slice.48
  101.5 1.6 reshape.129
  103.0 0.6 multiply_reduce_fusion.3
  103.7 0.6 mul.261
  104.3 1.0 copy-done.3
  105.3 0.3 multiply_convert_fusion.q_ref
  105.6 2.2 collective-permute-done
  107.8 6.3 %collective-permute-done.1 = bf16[512,512]{1,0:T(8,128)(2,1)} collective-permute-done((bf16[512,512]{1,0:T(8,128)(2,1)}, bf16[512,512]{1,0:T(8,128)(2,1)}, u32[]{:S(2)}, u32[]{:S(2)}) %collective-permute-start.1) | collective-permute-done | bytes 524320 | tf_op jit(solution)/shard_map/ppermute | solution.py:249
  114.1 1.3 maximum_maximum_fusion.kv_ref
  115.4 13.6 %attention.1 = (f32[512,512]{1,0:T(8,128)S(1)}, f32[1536,512]{1,0:T(8,128)}) custom-call(bf16[512,512]{1,0:T(8,128)(2,1)S(1)} %multiply_convert_fusion.q_ref, bf16[1536,512]{1,0:T(8,128)(2,1)S(1)} %maximum_maximum_fusion.kv_ref, bf16[512,512]{1,0:T(8,128)(2,1)S(1)} %copy-done, s32[512,1]{1,0:T(8,128)S(1)} %maximum_subtract_fusion.lo_ref), custom_call_target="tpu_custom_call" | custom-call | tf_op jit(solution)/shard_map/attention/pallas_call | solution.py:77
  129.0 1.3 reshape.131
  130.4 2.8 multiply_reduce_fusion.2
  133.2 2.1 convert.11
  135.3 0.1 fusion.17
  135.4 2.1 collective-permute-start.2
  137.4 1.3 collective-permute-start.3
  138.7 0.6 mul.289
  139.4 1.4 multiply_reduce_fusion.1
  140.7 9.8 %collective-permute-done.2 = bf16[512,512]{1,0:T(8,128)(2,1)S(1)} collective-permute-done((bf16[512,512]{1,0:T(8,128)(2,1)S(1)}, bf16[512,512]{1,0:T(8,128)(2,1)S(1)}, u32[]{:S(2)}, u32[]{:S(2)}) %collective-permute-start.2) | collective-permute-done | bytes 524320 | tf_op jit(solution)/shard_map/ppermute | solution.py:249
  150.6 3.9 %collective-permute-done.3 = bf16[512,512]{1,0:T(8,128)(2,1)S(1)} collective-permute-done((bf16[512,512]{1,0:T(8,128)(2,1)S(1)}, bf16[512,512]{1,0:T(8,128)(2,1)S(1)}, u32[]{:S(2)}, u32[]{:S(2)}) %collective-permute-start.3) | collective-permute-done | bytes 524320 | tf_op jit(solution)/shard_map/ppermute | solution.py:249
  154.5 1.4 convert_add_fusion
  155.9 0.8 slice.53
  156.7 0.7 slice.66
  157.5 2.1 reshape.132
  159.6 2.7 multiply_reduce_fusion.5
  162.3 0.6 mul.298
  162.9 0.2 multiply_reduce_fusion.4
  163.1 0.2 copy-done.9
  163.3 0.1 copy-done.19
  163.4 0.3 multiply_reduce_fusion
  163.7 1.2 pad_maximum_fusion.d
  164.9 85.8 %both_reductions.1 = (f32[2,336,512]{2,1,0:T(8,128)}, bf16[336,1024]{1,0:T(8,128)(2,1)}) custom-call(bf16[8,672,1024]{2,1,0:T(8,128)(2,1)} %bitcast.73, bf16[8,2,336,512]{3,2,1,0:T(8,128)(2,1)} %bitcast.72, bf16[512,1024]{1,0:T(8,128)(2,1)} %pad_maximum_fusion.d), custom_call_target="tpu_custom_call" | custom-call | tf_op jit(solution)/shard_map/both_reductions/pallas_call | solution.py:217
  250.7 1.9 fusion.18
  252.6 1.7 slice.45
  254.3 22.4 %psum.21 = f32[512]{0:T(512)S(1)} all-reduce(f32[512]{0:T(512)S(1)} %multiply_reduce_fusion), channel_id=1, replica_groups=mesh['ctx'=16,'fsdp'=8] {'fsdp'}, use_global_device_ids=true, to_apply=%region_8.9 | all-reduce | flops 512 | bytes 4096 | tf_op jit(solution)/shard_map/psum | solution.py:357
  276.7 0.6 broadcast_multiply_fusion.2
  277.3 1.2 fusion.9
  278.6 31.0 %all-reduce = bf16[672]{0:T(1024)(128)(2,1)S(1)} all-reduce(bf16[672]{0:T(1024)(128)(2,1)S(1)} %multiply_convert_fusion.2), channel_id=2, replica_groups=mesh['ctx'=16,'fsdp'=8] {'ctx'}, use_global_device_ids=true, to_apply=%region_10.11.clone | all-reduce | flops 672 | bytes 2688
  309.6 62.0 %all-reduce.1 = (f32[128]{0:T(128)}, f32[128]{0:T(128)}) all-reduce(f32[128]{0:T(128)S(1)} %get-tuple-element.33, f32[128]{0:T(128)S(1)} %get-tuple-element.32), channel_id=1, replica_groups=mesh['ctx'=16,'fsdp'=8] {'ctx','fsdp'}, use_global_device_ids=true, to_apply=%region_13.14 | all-reduce | flops 256 | bytes 2048 | tf_op jit(solution)/shard_map/psum | solution.py:367
  371.6 0.6 dynamic-slice_convert_fusion
  (60 shorter events, 0.3 us)
Async XLA Ops:
  7.2 71.3 %all-gather.2.cloned.1.call-start = ((), (), s32[]{:S(2)}) async-start(), calls=%async_computation | async-start | bytes 11698176 | tf_op jit(solution)/shard_map/all_gather | solution.py:293
  10.2 4.0 %copy-start.20 = (f32[5376]{0:T(1024)S(1)}, f32[5376]{0:T(1024)}, u32[]{:S(2)}) copy-start(f32[5376]{0:T(1024)} %param.14) | copy-start | bytes 64516
  10.4 4.2 %copy-start.1 = (bf16[512,5376]{1,0:T(8,128)(2,1)S(1)}, bf16[512,5376]{1,0:T(8,128)(2,1)}, u32[]{:S(2)}) copy-start(bf16[512,5376]{1,0:T(8,128)(2,1)} %param.9) | copy-start | bytes 16515076
  27.2 2.8 copy-start.23
  27.2 4.1 %copy-start.21 = (f32[128]{0:T(128)S(1)}, f32[128]{0:T(128)}, u32[]{:S(2)}) copy-start(f32[128]{0:T(128)} %param.16) | copy-start | bytes 1540
  27.2 4.1 %copy-start.22 = (f32[128]{0:T(128)S(1)}, f32[128]{0:T(128)}, u32[]{:S(2)}) copy-start(f32[128]{0:T(128)} %param.15) | copy-start | bytes 1540
  89.7 2.8 copy-start.13
  91.1 2.4 copy-start.6
  91.8 8.6 %copy-start.11 = (f32[512,2]{1,0:T(8,128)}, f32[512,2]{1,0:T(8,128)S(1)}, u32[]{:S(2)}) copy-start(f32[512,2]{1,0:T(8,128)S(1)} %add_rsqrt_fusion) | copy-start | bytes 12292
  92.4 8.0 %copy-start.7 = (f32[512,2,128]{2,1,0:T(2,128)}, f32[512,2,128]{2,1,0:T(2,128)S(1)}, u32[]{:S(2)}) copy-start(f32[512,2,128]{2,1,0:T(2,128)S(1)} %mul.271) | copy-start | bytes 1572868
  92.5 7.8 %copy-start.15 = (bf16[512,256]{1,0:T(8,128)(2,1)}, bf16[512,256]{1,0:T(8,128)(2,1)S(1)}, u32[]{:S(2)}) copy-start(bf16[512,256]{1,0:T(8,128)(2,1)S(1)} %multiply_convert_fusion.1) | copy-start | bytes 786436
  93.5 14.3 %collective-permute-start = (bf16[512,512]{1,0:T(8,128)(2,1)}, bf16[512,512]{1,0:T(8,128)(2,1)}, u32[]{:S(2)}, u32[]{:S(2)}) collective-permute-start(bf16[512,512]{1,0:T(8,128)(2,1)} %pad_maximum_fusion.2), channel_id=1, source_target_pairs={{0,16},{8,24},{16,32},{24,40},{32,48},{40,56},{48,64},{56,72},{64,... | collective-permute-start | bytes 1572872 | tf_op jit(solution)/shard_map/ppermute | solution.py:249
  97.3 16.8 %collective-permute-start.1 = (bf16[512,512]{1,0:T(8,128)(2,1)}, bf16[512,512]{1,0:T(8,128)(2,1)}, u32[]{:S(2)}, u32[]{:S(2)}) collective-permute-start(bf16[512,512]{1,0:T(8,128)(2,1)} %pad_maximum_fusion.2), channel_id=1, source_target_pairs={{0,8},{8,16},{16,24},{24,32},{32,40},{40,48},{48,56},{56,64},{64,7... | collective-permute-start | bytes 1572872 | tf_op jit(solution)/shard_map/ppermute | solution.py:249
  103.0 2.5 copy-start.2
  103.7 4.1 %copy-start.17 = (f32[512,4]{1,0:T(8,128)}, f32[512,4]{1,0:T(8,128)S(1)}, u32[]{:S(2)}) copy-start(f32[512,4]{1,0:T(8,128)S(1)} %add_rsqrt_fusion.1) | copy-start | bytes 24580
  103.7 10.4 %copy-start.14 = (bf16[512,256]{1,0:T(8,128)(2,1)S(1)}, bf16[512,256]{1,0:T(8,128)(2,1)}, u32[]{:S(2)}) copy-start(bf16[512,256]{1,0:T(8,128)(2,1)} %copy-done.13) | copy-start | bytes 786436
  103.7 10.4 %copy-start.16 = (bf16[512,256]{1,0:T(8,128)(2,1)S(1)}, bf16[512,256]{1,0:T(8,128)(2,1)}, u32[]{:S(2)}) copy-start(bf16[512,256]{1,0:T(8,128)(2,1)} %copy-done.15) | copy-start | bytes 786436
  104.3 1.0 copy-start.3
  105.6 9.9 %copy-start = (bf16[512,512]{1,0:T(8,128)(2,1)S(1)}, bf16[512,512]{1,0:T(8,128)(2,1)}, u32[]{:S(2)}) copy-start(bf16[512,512]{1,0:T(8,128)(2,1)} %do_ref.1) | copy-start | bytes 1572868
  129.0 1.3 copy-start.18
  135.3 4.1 %copy-start.4 = (f32[512,4,128]{2,1,0:T(4,128)S(1)}, f32[512,4,128]{2,1,0:T(4,128)}, u32[]{:S(2)}) copy-start(f32[512,4,128]{2,1,0:T(4,128)} %copy-done.3) | copy-start | bytes 3145732
  135.4 15.2 %collective-permute-start.2 = (bf16[512,512]{1,0:T(8,128)(2,1)S(1)}, bf16[512,512]{1,0:T(8,128)(2,1)S(1)}, u32[]{:S(2)}, u32[]{:S(2)}) collective-permute-start(bf16[512,512]{1,0:T(8,128)(2,1)S(1)} %get-tuple-element.22), channel_id=1, source_target_pairs={{8,0},{16,8},{24,16},{32,24},{40,32},{48,40},{56,48},{64,56},{72,6... | collective-permute-start | bytes 1572872 | tf_op jit(solution)/shard_map/ppermute | solution.py:249
  137.4 17.0 %collective-permute-start.3 = (bf16[512,512]{1,0:T(8,128)(2,1)S(1)}, bf16[512,512]{1,0:T(8,128)(2,1)S(1)}, u32[]{:S(2)}, u32[]{:S(2)}) collective-permute-start(bf16[512,512]{1,0:T(8,128)(2,1)S(1)} %get-tuple-element.23), channel_id=1, source_target_pairs={{16,0},{24,8},{32,16},{40,24},{48,32},{56,40},{64,48},{72,56},{80,... | collective-permute-start | bytes 1572872 | tf_op jit(solution)/shard_map/ppermute | solution.py:249
  155.9 3.7 copy-start.12
  159.6 3.3 copy-start.8
  162.3 1.0 copy-start.9
  162.3 1.1 copy-start.19
  164.9 112.5 %copy-start.10 = (bf16[512,672]{0,1:T(8,128)(2,1)S(1)}, bf16[512,672]{0,1:T(8,128)(2,1)}, u32[]{:S(2)}) copy-start(bf16[512,672]{0,1:T(8,128)(2,1)} %copy.32) | copy-start | bytes 2064388
  250.7 26.6 %copy-start.5 = (f32[2,336,512]{2,1,0:T(8,128)S(1)}, f32[2,336,512]{2,1,0:T(8,128)}, u32[]{:S(2)}) copy-start(f32[2,336,512]{2,1,0:T(8,128)} %get-tuple-element.14) | copy-start | bytes 4128772
Sparse Core Ops, SparseCore 0:
  10.3 68.1 all-gather.1
